TPU v7x, 32 devices: a whole 2x2x4 slice. The times are simulated.
32 devices in a mesh: grp: 2 (over x), req: 16 (over z, y, core).
Axes of the slice: x: 2, y: 2, z: 4, core: 2. Of those that a mesh axis runs over, the one named last changes fastest.
Arguments:
- tokens: bfloat16 [16384, 8192], P(('grp', 'req')), parts along dimension 0, may hold values from -6 to 6
- key_value_weight: bfloat16 [8192, 1024], P('req'), may hold values from -0.0625 to 0.0625
- adapter_down_weight: bfloat16 [64, 8192, 16], P(None, 'req'), may hold values from -0.0625 to 0.0625
- adapter_up_weight: bfloat16 [64, 1024, 16], P(None, 'req'), may hold values from -1.5 to 1.5
- request_adapter: int32 [64], P('grp'), parts along dimension 0, may hold values from 0 to 63
- adapter_table_row: int32 [64], replicated, may hold values from 0 to 63, each once
- lengths: int32 [64], P(('grp', 'req')), parts along dimension 0, may hold values from 1 to 256, as said below
Outputs:
- kv_out: bfloat16 [16384, 1024], P(('grp', 'req')), parts along dimension 0
There are 2 independent parts, one for each index of `grp`. A program takes and returns all parts, laid end to end along the dimension named above; an argument that names none is the same for every part. Nothing has to cross between parts.
Inputs may be any that keep to these rules, and one draw needn't show every extreme that they name: `lengths`: some request has exactly 256 live rows.
All inputs are finite; a program needn't handle non-finite values.
Results may differ from a plain program's by a relative error of at most 0.003.
Values may be sent and summed in bfloat16 or wider, within the bound.
A program may use at most 128 MiB of HBM per device.

v0:
```python
import jax
import jax.numpy as jnp
from jax import lax
from jax.sharding import PartitionSpec as P


def body(
    tokens,
    key_value_weight,
    adapter_down_weight,
    adapter_up_weight,
    request_adapter,
    adapter_table_row,
    lengths,
):
    per_device = lengths.shape[0]
    row_span = tokens.shape[0] // per_device
    width = tokens.shape[1]
    slot_rows = adapter_table_row[request_adapter]
    base_part = jnp.dot(
        tokens,
        lax.all_gather(key_value_weight, "req", axis=0, tiled=True),
        preferred_element_type=jnp.float32,
    )
    down_transfer = adapter_down_weight[slot_rows]
    up_transfer = adapter_up_weight[slot_rows]
    down_maps, up_maps = (
        lax.all_to_all(down_transfer, "req", split_axis=0, concat_axis=1, tiled=True),
        lax.all_to_all(up_transfer, "req", split_axis=0, concat_axis=1, tiled=True),
    )
    grouped = tokens.reshape(per_device, row_span, width)
    reduced = jnp.einsum(
        "qtd,qdk->qtk", grouped, down_maps, preferred_element_type=jnp.float32
    ).astype(jnp.bfloat16)
    adapter_term = jnp.einsum("qtk,qwk->qtw", reduced, up_maps, preferred_element_type=jnp.float32)
    adapter_term = adapter_term.reshape(tokens.shape[0], key_value_weight.shape[1])
    position = jnp.arange(row_span, dtype=jnp.int32)
    live_rows = (position[None, :] < lengths[:, None]).reshape(tokens.shape[0], 1)
    mixed = jnp.where(live_rows, base_part + 0.5 * adapter_term, jnp.zeros_like(base_part))
    return mixed.astype(jnp.bfloat16)


def solution(mesh):
    placed = (
        P(("grp", "req"), None),
        P("req", None),
        P(None, "req", None),
        P(None, "req", None),
        P("grp"),
        P(),
        P(("grp", "req")),
    )
    return jax.shard_map(
        body, mesh=mesh, in_specs=placed, out_specs=P(("grp", "req"), None), check_vma=False
    )
```

profile of v0, /device:TPU:1, one launch (start us, length us, event | category | flops | bytes accessed | tf_op | source)
XLA Modules:
  0.0 172.5 jit_solution(12574115646161947593)
XLA Ops:
  6.5 0.0 copy-start
  6.5 0.0 copy-start.1
  6.5 0.0 all-gather.2.cloned.1.call-start
  6.5 0.7 all-gather.2.cloned.1.call-update
  7.3 0.7 compare_select_fusion.1
  7.9 1.4 gather_fusion
  9.3 1.5 gather_fusion.2
  10.8 0.8 reshape.61
  11.6 7.3 %all-to-all-start.1 = ((bf16[16,2,1024]{2,1,0:T(2,128)(2,1)}), bf16[16,2,1024]{2,1,0:T(2,128)(2,1)S(1)}, u32[]{:S(2)}, u32[]{:S(2)}) async-start(bf16[16,2,1024]{2,1,0:T(2,128)(2,1)} %reshape.61), calls=%async_computation.1 | async-start | bytes 131072 | tf_op jit(solution)/shard_map/all_to_all | solution.py:29
  19.0 0.0 copy-done
  19.0 1.4 gather_fusion.1
  20.3 4.7 %all-to-all-done.1 = bf16[16,2,1024]{2,1,0:T(2,128)(2,1)S(1)} async-done(((bf16[16,2,1024]{2,1,0:T(2,128)(2,1)}), bf16[16,2,1024]{2,1,0:T(2,128)(2,1)S(1)}, u32[]{:S(2)}, u32[]{:S(2)}) %all-to-all-start.1) | async-done | bytes 65568 | tf_op jit(solution)/shard_map/all_to_all | solution.py:29
  25.0 4.3 %all-to-all-start = ((bf16[32,512,16]{1,2,0:T(8,128)(2,1)}), bf16[32,512,16]{1,2,0:T(8,128)(2,1)S(1)}, u32[]{:S(2)}, u32[]{:S(2)}) async-start(bf16[32,512,16]{1,2,0:T(8,128)(2,1)} %gather_fusion.1), calls=%async_computation | async-start | bytes 1048576 | tf_op jit(solution)/shard_map/all_to_all | solution.py:28
  29.3 0.0 copy-done.1
  29.3 0.1 iota_compare_fusion
  29.4 0.1 reshape.62
  29.6 0.1 copy.14
  29.6 0.1 all_to_all.33
  29.8 21.8 %all-to-all-done = bf16[32,512,16]{1,2,0:T(8,128)(2,1)S(1)} async-done(((bf16[32,512,16]{1,2,0:T(8,128)(2,1)}), bf16[32,512,16]{1,2,0:T(8,128)(2,1)S(1)}, u32[]{:S(2)}, u32[]{:S(2)}) %all-to-all-start) | async-done | bytes 524320 | tf_op jit(solution)/shard_map/all_to_all | solution.py:28
  51.6 0.3 copy.13
  51.9 1.0 all_to_all.29
  52.9 6.3 %convolution_multiply_fusion = f32[2,256,1024]{2,1,0:T(8,128)S(1)} fusion(bf16[2,1024,16]{1,2,0:T(8,128)(2,1)S(1)} %all_to_all.33, bf16[2,8192,16]{1,2,0:T(8,128)(2,1)} %all_to_all.29, bf16[2,256,8192]{2,1,0:T(8,128)(2,1)} %bitcast.34), kind=kOutput, calls=%fused_computation.6 | convolution fusion | flops 151527424 | bytes 11075584 | tf_op jit(solution)/shard_map/qtk,qwk->qtw/dot_general | solution.py:35
  59.3 90.8 %all-gather.2.cloned.1.call-done = bf16[8192,1024]{1,0:T(8,128)(2,1)} async-done(((bf16[512,1024]{1,0:T(8,128)(2,1)}), bf16[8192,1024]{1,0:T(8,128)(2,1)}) %all-gather.2.cloned.1.call-update) | async-done | bytes 16777232 | tf_op jit(solution)/shard_map/all_gather | solution.py:22
  150.1 15.6 %fusion.1 = bf16[512,1024]{1,0:T(8,128)(2,1)} fusion(f32[2,256,1024]{2,1,0:T(8,128)S(1)} %convolution_multiply_fusion, bf16[512,8192]{1,0:T(8,128)(2,1)} %param.7, bf16[8192,1024]{1,0:T(8,128)(2,1)} %all-gather.2.cloned.1.call-done, pred[512]{0:T(512)(128)(4,1)S(1)} %lt.37), kind=kOutput, calls=%fused_computation.5 | convolution fusion | flops 8591507456 | bytes 28312064 | tf_op jit(solution)/shard_map/dot_general | solution.py:20
  (4 shorter events, 0.0 us)
Async XLA Ops:
  6.5 12.4 %copy-start = (bf16[64,512,16]{1,2,0:T(8,128)(2,1)S(1)}, bf16[64,512,16]{1,2,0:T(8,128)(2,1)}, u32[]{:S(2)}) copy-start(bf16[64,512,16]{1,2,0:T(8,128)(2,1)} %param.9) | copy-start | bytes 3145732
  6.5 22.8 %copy-start.1 = (s32[2]{0:T(128)S(1)}, s32[2]{0:T(128)}, u32[]{:S(2)}) copy-start(s32[2]{0:T(128)} %param.13) | copy-start | bytes 28
  6.5 143.5 %all-gather.2.cloned.1.call-start = ((), (), s32[]{:S(2)}) async-start(), calls=%async_computation.2 | async-start | bytes 17825792 | tf_op jit(solution)/shard_map/all_gather | solution.py:22
  11.6 13.4 %all-to-all-start.1 = ((bf16[16,2,1024]{2,1,0:T(2,128)(2,1)}), bf16[16,2,1024]{2,1,0:T(2,128)(2,1)S(1)}, u32[]{:S(2)}, u32[]{:S(2)}) async-start(bf16[16,2,1024]{2,1,0:T(2,128)(2,1)} %reshape.61), calls=%async_computation.1 | async-start | bytes 131072 | tf_op jit(solution)/shard_map/all_to_all | solution.py:29
  25.0 26.6 %all-to-all-start = ((bf16[32,512,16]{1,2,0:T(8,128)(2,1)}), bf16[32,512,16]{1,2,0:T(8,128)(2,1)S(1)}, u32[]{:S(2)}, u32[]{:S(2)}) async-start(bf16[32,512,16]{1,2,0:T(8,128)(2,1)} %gather_fusion.1), calls=%async_computation | async-start | bytes 1048576 | tf_op jit(solution)/shard_map/all_to_all | solution.py:28
Sparse Core Ops, SparseCore 0:
  9.5 140.4 all-gather.1
where the time goes:
time: 173 us; the launch traced here: 172 us
  waiting for transfers between devices  118 us (68%)
  matrix products  21.9 us (13%)
  between operations  13.4 us (8%)
  starting transfers between devices  11.7 us (7%)
  local copies, waits for them, and re-layouts  6.74 us (4%)
    all_gather x1, waiting for transfers between devices, body(): lax.all_gather(key_value_weight, 'req', axis=0, tiled=True)  90.8 us
    all_to_all x1, waiting for transfers between devices, body(): lax.all_to_all(down_transfer, 'req', split_axis=0, concat_axis=1, tiled=T...  21.8 us
    dot_general x1, matrix products, body(): jnp.dot(tokens, lax.all_gather(key_value_weight, 'req', axis=0, tiled=Tru...  15.6 us
    all_to_all x1, starting transfers between devices, body(): lax.all_to_all(up_transfer, 'req', split_axis=0, concat_axis=1, tiled=True)  7.35 us
    dot_general x1, matrix products, body(): jnp.einsum('qtk,qwk->qtw', reduced, up_maps, preferred_element_type=jnp.f...  6.34 us
    all_to_all x1, waiting for transfers between devices, body(): lax.all_to_all(up_transfer, 'req', split_axis=0, concat_axis=1, tiled=True)  4.67 us
    all_to_all x1, starting transfers between devices, body(): lax.all_to_all(down_transfer, 'req', split_axis=0, concat_axis=1, tiled=T...  4.32 us
  transfers between devices with their start and end apart: 3, of which 3 were waited for; matrix products, arithmetic and copies ran while one was open for 7% of the time, Pallas kernels for 0%

commit v1 on v0

--- a/solution.py
+++ b/solution.py
@@ -1,10 +1,345 @@
 import jax
 import jax.numpy as jnp
 from jax import lax
+from jax.experimental import pallas as pl
+from jax.experimental.pallas import tpu as pltpu
 from jax.sharding import PartitionSpec as P
 
-
-def body(
+MESH = pl.DeviceIdType.MESH
+
+
+def gather_kernel(
+    req_ref, table_ref, tok_hbm, w_hbm, down_hbm, up_hbm, out_ref,
+    wfull, tok, acc, down_tab, up_tab, down_stage, up_stage, down_in, up_in, up_all, red,
+    local_sem, recv_sem, send_sem, ad_send, ad_recv,
+):
+    depth, width = w_hbm.shape
+    rows = tok.shape[0]
+    per = req_ref.shape[0] // 16
+    rank = down_tab.shape[1]
+    side = depth * 3 // 8
+    mid = depth - 2 * side
+    x = lax.axis_index("grp")
+    me = lax.axis_index("req")
+    c = lax.rem(me, 2)
+    y = lax.rem(lax.div(me, 2), 2)
+    z = lax.div(me, 4)
+    flip = lax.div(z, 2)
+    zz = z + flip * (3 - 2 * z)
+    inner = z + 1 - 2 * flip
+    outer = z - 1 + 2 * flip
+    inside = zz == 1
+    order = []
+    for o in (zz, 1 - zz, 2, 3):
+        order.append(o + flip * (3 - 2 * o))
+
+    def chip(far, k):
+        yy = (1 - y) if far else y
+        return order[k] * 2 + yy
+
+    def device(xx, yy, zz_, cc):
+        return (xx, (zz_ * 2 + yy) * 2 + cc)
+
+    z_in = device(x, y, inner, c)
+    z_out = device(x, y, outer, c)
+    y_dev = device(x, 1 - y, z, c)
+    x_dev = device(1 - x, y, z, c)
+    sib = device(x, y, z, 1 - c)
+
+    tok_copy = pltpu.make_async_copy(tok_hbm, tok, local_sem.at[0])
+    own_rows = wfull.at[chip(0, 0), pl.ds(pl.multiple_of(c * depth, depth), depth)]
+    own_copy = pltpu.make_async_copy(w_hbm, own_rows, local_sem.at[1])
+    down_copy = pltpu.make_async_copy(down_hbm, down_tab, local_sem.at[2])
+    up_copy = pltpu.make_async_copy(up_hbm, up_tab, local_sem.at[3])
+    down_copy.start()
+    up_copy.start()
+    own_copy.start()
+    tok_copy.start()
+
+    barrier = pltpu.get_barrier_semaphore()
+
+    def greet(i, carry):
+        pl.semaphore_signal(
+            barrier, inc=1, device_id=(x, lax.rem(me + i, 16)), device_id_type=MESH
+        )
+        return carry
+
+    lax.fori_loop(1, 16, greet, 0)
+    pl.semaphore_signal(barrier, inc=1, device_id=x_dev, device_id_type=MESH)
+    pl.semaphore_wait(barrier, 16)
+
+    starts = (x * (side + mid), side, (1 - x) * (side + mid))
+    counts = (side, mid, side)
+    pending = []
+
+    def piece(part, m, cc):
+        at = pl.multiple_of(cc * depth + starts[part], 64)
+        return wfull.at[m, pl.ds(at, counts[part])]
+
+    def send(part, m, dev, landing=None, own=False, when=None):
+        here = piece(part, m, c)
+        if own:
+            src = w_hbm.at[pl.ds(pl.multiple_of(starts[part], 64), counts[part])]
+        else:
+            src = here
+        copy = pltpu.make_async_remote_copy(
+            src_ref=src,
+            dst_ref=here,
+            send_sem=send_sem.at[len(pending)],
+            recv_sem=recv_sem.at[part if landing is None else landing, m, c],
+            device_id=dev,
+            device_id_type=MESH,
+        )
+        pending.append((copy, when))
+        if when is None:
+            copy.start()
+        else:
+            pl.when(when)(copy.start)
+
+    def arrived(part, m, cc):
+        here = piece(part, m, cc)
+        pltpu.make_async_remote_copy(
+            src_ref=here,
+            dst_ref=here,
+            send_sem=send_sem.at[0],
+            recv_sem=recv_sem.at[part, m, cc],
+            device_id=sib,
+            device_id_type=MESH,
+        ).wait_recv()
+
+    def multiply(m):
+        cols = pl.ds(pl.multiple_of(m * 2 * depth, 2 * depth), 2 * depth)
+
+        def tile(j, carry):
+            at = pl.ds(pl.multiple_of(j * 256, 256), 256)
+            acc[:, at] += jnp.dot(
+                tok[:, cols], wfull[m, :, at], preferred_element_type=jnp.float32
+            )
+            return carry
+
+        lax.fori_loop(0, width // 256, tile, 0)
+
+    def sibling_done(m):
+        for part in range(3):
+            arrived(part, m, 1 - c)
+
+    mine = chip(0, 0)
+    for part in (0, 1):
+        send(part, mine, z_in, own=True)
+        send(part, mine, z_out, own=True, when=inside)
+        send(part, mine, y_dev, own=True)
+    for part in range(3):
+        send(part, mine, sib, own=True)
+
+    down_copy.wait()
+    up_copy.wait()
+
+    def pick(q, carry):
+        row = table_ref[req_ref[q]]
+        down_stage[q] = down_tab[row]
+        up_stage[q] = up_tab[row]
+        return carry
+
+    lax.fori_loop(0, per * 16, pick, 0)
+
+    def adapter_copies(i, dest, source):
+        to = pl.ds(dest * per, per)
+        return (
+            pltpu.make_async_remote_copy(
+                src_ref=down_stage.at[to],
+                dst_ref=down_in.at[source],
+                send_sem=ad_send.at[0, i],
+                recv_sem=ad_recv.at[0, source],
+                device_id=(x, dest),
+                device_id_type=MESH,
+            ),
+            pltpu.make_async_remote_copy(
+                src_ref=up_stage.at[to],
+                dst_ref=up_in.at[source],
+                send_sem=ad_send.at[1, i],
+                recv_sem=ad_recv.at[1, source],
+                device_id=(x, dest),
+                device_id_type=MESH,
+            ),
+        )
+
+    def ship(i, carry):
+        for copy in adapter_copies(i, lax.rem(me + i, 16), me):
+            copy.start()
+        return carry
+
+    lax.fori_loop(1, 16, ship, 0)
+    down_in[me] = down_stage[pl.ds(me * per, per)]
+    up_in[me] = up_stage[pl.ds(me * per, per)]
+    acc[...] = jnp.zeros_like(acc)
+    red[...] = jnp.zeros_like(red)
+    own_copy.wait()
+    tok_copy.wait()
+
+    def adapters():
+        def landed(i, carry):
+            for copy in adapter_copies(i, me, lax.rem(me + 16 - i, 16)):
+                copy.wait_recv()
+            return carry
+
+        lax.fori_loop(1, 16, landed, 0)
+
+        def reduce(s, carry):
+            cols = pl.ds(pl.multiple_of(s * depth, depth), depth)
+            red[...] += lax.dot_general(
+                tok[:, cols],
+                down_in[s].reshape(per * rank, depth),
+                (((1,), (1,)), ((), ())),
+                preferred_element_type=jnp.float32,
+            )
+            return carry
+
+        lax.fori_loop(0, 16, reduce, 0)
+        span = rows // per
+        row_request = lax.broadcasted_iota(jnp.int32, red.shape, 0) // span
+        map_request = lax.broadcasted_iota(jnp.int32, red.shape, 1) // rank
+        kept = jnp.where(row_request == map_request, red[...], 0.0).astype(jnp.bfloat16)
+        part = up_in.shape[3]
+        for s in range(0, 16, 2):
+            pair = [up_in[s + j].reshape(per * rank, part) for j in range(2)]
+            up_all[:, s * part:(s + 2) * part] = jnp.concatenate(pair, axis=1)
+
+        def tile(j, carry):
+            at = pl.ds(pl.multiple_of(j * 256, 256), 256)
+            acc[:, at] += 0.5 * jnp.dot(
+                kept, up_all[:, at], preferred_element_type=jnp.float32
+            )
+            return carry
+
+        lax.fori_loop(0, width // 256, tile, 0)
+
+    def from_x(far, k):
+        m = chip(far, k)
+        arrived(2, m, c)
+        send(2, m, sib)
+
+    for k in range(1, 4):
+        near, other = chip(0, k), chip(1, k - 1)
+        for part in (0, 1):
+            arrived(part, near, c)
+            if k == 1:
+                send(part, near, z_in, when=inside)
+            else:
+                send(part, near, z_out, when=inside)
+            send(part, near, y_dev)
+            if part == 0:
+                send(part, near, x_dev, landing=2)
+            send(part, near, sib)
+            arrived(part, other, c)
+            if part == 0:
+                send(part, other, x_dev, landing=2)
+            send(part, other, sib)
+        if k > 1:
+            from_x(0, k - 1)
+            from_x(1, k - 2)
+        if k == 1:
+            sibling_done(mine)
+            multiply(mine)
+        elif k == 2:
+            adapters()
+        else:
+            for far, j in ((0, 1), (1, 0)):
+                sibling_done(chip(far, j))
+                multiply(chip(far, j))
+    last = chip(1, 3)
+    arrived(0, last, c)
+    send(0, last, x_dev, landing=2)
+    send(0, last, sib)
+    arrived(1, last, c)
+    send(1, last, sib)
+    for far, j in ((0, 3), (1, 2)):
+        from_x(far, j)
+    for far, j in ((0, 2), (1, 1), (0, 3), (1, 2)):
+        sibling_done(chip(far, j))
+        multiply(chip(far, j))
+    from_x(1, 3)
+    sibling_done(last)
+    cols = pl.ds(pl.multiple_of(last * 2 * depth, 2 * depth), 2 * depth)
+
+    def finish(j, carry):
+        at = pl.ds(pl.multiple_of(j * 256, 256), 256)
+        total = acc[:, at] + jnp.dot(
+            tok[:, cols], wfull[last, :, at], preferred_element_type=jnp.float32
+        )
+        out_ref[:, at] = total.astype(out_ref.dtype)
+        return carry
+
+    lax.fori_loop(0, width // 256, finish, 0)
+
+    for copy, when in pending:
+        if when is None:
+            copy.wait_send()
+        else:
+            pl.when(when)(copy.wait_send)
+
+    def sent(i, carry):
+        for copy in adapter_copies(i, lax.rem(me + i, 16), me):
+            copy.wait_send()
+        return carry
+
+    lax.fori_loop(1, 16, sent, 0)
+
+
+def fused_body(tokens, weight, down, up, request_adapter, adapter_table_row, lengths):
+    rows, model = tokens.shape
+    depth, width = weight.shape
+    per = lengths.shape[0]
+    rank = down.shape[2]
+    adapters = down.shape[0]
+    requests = request_adapter.shape[0]
+    part = up.shape[1]
+    bf16 = jnp.bfloat16
+    any_space = pl.BlockSpec(memory_space=pl.ANY)
+    scalars = pl.BlockSpec(memory_space=pltpu.SMEM)
+    out = pl.pallas_call(
+        gather_kernel,
+        out_shape=jax.ShapeDtypeStruct((rows, width), bf16),
+        in_specs=[scalars, scalars] + [any_space] * 4,
+        out_specs=pl.BlockSpec(memory_space=pltpu.VMEM),
+        scratch_shapes=[
+            pltpu.VMEM((8, 2 * depth, width), bf16),
+            pltpu.VMEM((rows, model), bf16),
+            pltpu.VMEM((rows, width), jnp.float32),
+            pltpu.VMEM((adapters, rank, depth), bf16),
+            pltpu.VMEM((adapters, rank, part), bf16),
+            pltpu.VMEM((requests, rank, depth), bf16),
+            pltpu.VMEM((requests, rank, part), bf16),
+            pltpu.VMEM((16, per, rank, depth), bf16),
+            pltpu.VMEM((16, per, rank, part), bf16),
+            pltpu.VMEM((per * rank, width), bf16),
+            pltpu.VMEM((rows, per * rank), jnp.float32),
+            pltpu.SemaphoreType.DMA((4,)),
+            pltpu.SemaphoreType.DMA((3, 8, 2)),
+            pltpu.SemaphoreType.DMA((72,)),
+            pltpu.SemaphoreType.DMA((2, 16)),
+            pltpu.SemaphoreType.DMA((2, 16)),
+        ],
+        compiler_params=pltpu.CompilerParams(
+            collective_id=0, has_side_effects=True, vmem_limit_bytes=52 * 2**20
+        ),
+        cost_estimate=pl.CostEstimate(
+            flops=2 * rows * model * width, bytes_accessed=2 * rows * model, transcendentals=0
+        ),
+    )(
+        request_adapter,
+        adapter_table_row,
+        tokens,
+        weight,
+        jnp.swapaxes(down, 1, 2),
+        jnp.swapaxes(up, 1, 2),
+    )
+    span = rows // per
+    place = jnp.arange(span, dtype=jnp.int32)
+    live = (place[None, :] < lengths[:, None]).reshape(rows, 1)
+    return jnp.where(live, out, jnp.zeros_like(out))
+
+
+def plain_body(
     tokens,
     key_value_weight,
     adapter_down_weight,
@@ -50,6 +385,11 @@
         P(),
         P(("grp", "req")),
     )
+    routed = mesh.shape["grp"] == 2 and mesh.shape["req"] == 16
     return jax.shard_map(
-        body, mesh=mesh, in_specs=placed, out_specs=P(("grp", "req"), None), check_vma=False
-    )
+        fused_body if routed else plain_body,
+        mesh=mesh,
+        in_specs=placed,
+        out_specs=P(("grp", "req"), None),
+        check_vma=False,
+    )

time: 173 us -> 96.6 us (0.56)
  waiting for transfers between devices: 118 us -> 0 us
  Pallas kernels: 0 us -> 92.3 us
  matrix products: 21.9 us -> 0 us
  between operations: 13.4 us -> 0.01 us
  starting transfers between devices: 11.7 us -> 0 us
  local copies, waits for them, and re-layouts: 6.74 us -> 2.28 us
    pallas_call x0 -> x1, Pallas kernels: none -> 92.3 us  [fused_body(): pl.pallas_call(gather_kernel, out_shape=jax.ShapeDtypeStruct((rows, width...]
    all_gather x1 -> x0, waiting for transfers between devices: 90.8 us -> none  [body(): lax.all_gather(key_value_weight, 'req', axis=0, tiled=True)]
    all_to_all x2 -> x0, waiting for transfers between devices: 26.5 us -> none  [the longest x1 21.8 us: body(): lax.all_to_all(down_transfer, 'req', split_axis=0, concat_axis=1, tiled=T...]
    dot_general x2 -> x0, matrix products: 21.9 us -> none  [the longest x1 15.6 us: body(): jnp.dot(tokens, lax.all_gather(key_value_weight, 'req', axis=0, tiled=Tru...]
    all_to_all x2 -> x0, starting transfers between devices: 11.7 us -> none  [the longest x1 7.35 us: body(): lax.all_to_all(up_transfer, 'req', split_axis=0, concat_axis=1, tiled=True)]
    gather x3 -> x0, local copies, waits for them, and re-layouts: 4.27 us -> none  [the longest x1 1.54 us: body(): up_transfer = adapter_up_weight[slot_rows]]
  transfers between devices with their start and end apart: 3 -> 0, of which waited for: 3 -> 0; matrix products, arithmetic and copies ran while one was open for 7% -> 0% of each run, Pallas kernels for 0% -> 0%
where the time goes in v1:
time: 96.6 us; the launch traced here: 96.5 us
  Pallas kernels  92.3 us (96%)
  local copies, waits for them, and re-layouts  2.28 us (2%)
  other arithmetic  1.84 us (2%)
    pallas_call x1, Pallas kernels, fused_body(): pl.pallas_call(gather_kernel, out_shape=jax.ShapeDtypeStruct((rows, width...  92.3 us
    unnamed x6, local copies, waits for them, and re-layouts  2.26 us

profile of v1, /device:TPU:1, one launch (start us, length us, event | category | flops | bytes accessed | tf_op | source)
XLA Modules:
  0.0 96.5 jit_solution(15909153597424705132)
XLA Ops:
  0.0 0.7 iota_compare_fusion
  0.7 0.0 copy-start
  0.7 0.9 copy-done
  1.7 0.0 copy-start.1
  1.7 0.7 copy-done.1
  2.4 0.0 copy-start.2
  2.4 0.7 copy-done.2
  3.0 92.3 %shard_map.73 = bf16[512,1024]{1,0:T(8,128)(2,1)S(1)} custom-call(s32[32]{0:T(128)S(1)} %copy-done.1, s32[64]{0:T(128)S(1)} %copy-done.2, bf16[512,8192]{1,0:T(8,128)(2,1)} %tok_hbm.1, bf16[512,1024]{1,0:T(8,128)(2,1)} %w_hbm.1, bf16[64,16,512]{2,1,0:T(8,128)(2,1)} %bitcast.3, bf16[64,16,64]{2,1,0:T(8,128)(2,1)S(1)} %bitcast.2), custom_call_target="tpu_custom_call" | custom-call | flops 8589934592 | bytes 8388608 | tf_op jit(solution)/shard_map/pallas_call | solution.py:299
  95.3 1.1 %broadcast_select_fusion = bf16[512,1024]{1,0:T(8,128)(2,1)} fusion(bf16[512,1024]{1,0:T(8,128)(2,1)S(1)} %shard_map.73, pred[512]{0:T(512)(128)(4,1)S(1)} %lt.23), kind=kLoop, calls=%fused_computation | loop fusion | flops 524288 | bytes 2097664 | tf_op jit(solution)/shard_map/jit(_where)/select_n | solution.py:339
  (1 shorter events, 0.0 us)
Async XLA Ops:
  0.7 0.9 copy-start
  1.7 0.7 copy-start.1
  2.4 0.7 copy-start.2

commit v2 on v1

--- a/solution.py
+++ b/solution.py
@@ -6,10 +6,17 @@
 from jax.sharding import PartitionSpec as P
 
 MESH = pl.DeviceIdType.MESH
+SLOTS = 8
+SIDE = 3
+SHIP = 3
+VM = 60
+REDUCE = ((12, (0, 8)), (17, (8, 16)), (18, None))
+SENDS = 32 * SLOTS
 
 
 def gather_kernel(
-    req_ref, table_ref, tok_hbm, w_hbm, down_hbm, up_hbm, out_ref,
+    req_hbm, table_hbm, len_hbm, tok_hbm, w_hbm, down_hbm, up_hbm, out_ref,
+    req_ref, table_ref, len_ref,
     wfull, tok, acc, down_tab, up_tab, down_stage, up_stage, down_in, up_in, up_all, red,
     local_sem, recv_sem, send_sem, ad_send, ad_recv,
 ):
@@ -17,8 +24,11 @@
     rows = tok.shape[0]
     per = req_ref.shape[0] // 16
     rank = down_tab.shape[1]
-    side = depth * 3 // 8
-    mid = depth - 2 * side
+    len_count = len_hbm.shape[0]
+    tile_width = width // 4
+    strip = depth // SLOTS
+    side = SIDE
+    mid = SLOTS - 2 * side
     x = lax.axis_index("grp")
     me = lax.axis_index("req")
     c = lax.rem(me, 2)
@@ -51,6 +61,14 @@
     own_copy = pltpu.make_async_copy(w_hbm, own_rows, local_sem.at[1])
     down_copy = pltpu.make_async_copy(down_hbm, down_tab, local_sem.at[2])
     up_copy = pltpu.make_async_copy(up_hbm, up_tab, local_sem.at[3])
+    scalar_copies = [
+        pltpu.make_async_copy(src, dst, local_sem.at[4 + i])
+        for i, (src, dst) in enumerate(
+            ((req_hbm, req_ref), (table_hbm, table_ref), (len_hbm, len_ref))
+        )
+    ]
+    for copy in scalar_copies:
+        copy.start()
     down_copy.start()
     up_copy.start()
     own_copy.start()
@@ -68,69 +86,70 @@
     pl.semaphore_signal(barrier, inc=1, device_id=x_dev, device_id_type=MESH)
     pl.semaphore_wait(barrier, 16)
 
-    starts = (x * (side + mid), side, (1 - x) * (side + mid))
-    counts = (side, mid, side)
     pending = []
 
-    def piece(part, m, cc):
-        at = pl.multiple_of(cc * depth + starts[part], 64)
-        return wfull.at[m, pl.ds(at, counts[part])]
-
-    def send(part, m, dev, landing=None, own=False, when=None):
-        here = piece(part, m, c)
-        if own:
-            src = w_hbm.at[pl.ds(pl.multiple_of(starts[part], 64), counts[part])]
-        else:
-            src = here
-        copy = pltpu.make_async_remote_copy(
-            src_ref=src,
-            dst_ref=here,
-            send_sem=send_sem.at[len(pending)],
-            recv_sem=recv_sem.at[part if landing is None else landing, m, c],
-            device_id=dev,
-            device_id_type=MESH,
-        )
+    def piece(slot, m, cc):
+        at = pl.multiple_of(cc * depth + slot * strip, strip)
+        return wfull.at[m, pl.ds(at, strip)]
+
+    def begin(copy, when):
         pending.append((copy, when))
         if when is None:
             copy.start()
         else:
             pl.when(when)(copy.start)
 
-    def arrived(part, m, cc):
-        here = piece(part, m, cc)
+    def send(slot, m, dev, own=False, when=None):
+        here = piece(slot, m, c)
+        src = w_hbm.at[pl.ds(pl.multiple_of(slot * strip, strip), strip)] if own else here
+        copy = pltpu.make_async_remote_copy(
+            src_ref=src,
+            dst_ref=here,
+            send_sem=send_sem.at[len(pending)],
+            recv_sem=recv_sem.at[slot, m, c],
+            device_id=dev,
+            device_id_type=MESH,
+        )
+        begin(copy, when)
+
+    def arrived(slot, m, cc):
+        here = piece(slot, m, cc)
         pltpu.make_async_remote_copy(
             src_ref=here,
             dst_ref=here,
             send_sem=send_sem.at[0],
-            recv_sem=recv_sem.at[part, m, cc],
+            recv_sem=recv_sem.at[slot, m, cc],
             device_id=sib,
             device_id_type=MESH,
         ).wait_recv()
 
-    def multiply(m):
-        cols = pl.ds(pl.multiple_of(m * 2 * depth, 2 * depth), 2 * depth)
-
-        def tile(j, carry):
-            at = pl.ds(pl.multiple_of(j * 256, 256), 256)
-            acc[:, at] += jnp.dot(
-                tok[:, cols], wfull[m, :, at], preferred_element_type=jnp.float32
-            )
-            return carry
-
-        lax.fori_loop(0, width // 256, tile, 0)
+    def share_own(m, cc):
+        return pltpu.make_async_remote_copy(
+            src_ref=w_hbm,
+            dst_ref=wfull.at[m, pl.ds(pl.multiple_of(cc * depth, depth), depth)],
+            send_sem=send_sem.at[len(pending)],
+            recv_sem=recv_sem.at[0, m, cc],
+            device_id=sib,
+            device_id_type=MESH,
+        )
 
     def sibling_done(m):
-        for part in range(3):
-            arrived(part, m, 1 - c)
+        for slot in range(SLOTS):
+            arrived(slot, m, 1 - c)
+
+    sides = [x * (side + mid) + j for j in range(side)]
+    others = [(1 - x) * (side + mid) + j for j in range(side)]
+    middle = [side + j for j in range(mid)]
 
     mine = chip(0, 0)
-    for part in (0, 1):
-        send(part, mine, z_in, own=True)
-        send(part, mine, z_out, own=True, when=inside)
-        send(part, mine, y_dev, own=True)
-    for part in range(3):
-        send(part, mine, sib, own=True)
-
+    for slot in sides + middle:
+        send(slot, mine, z_in, own=True)
+        send(slot, mine, z_out, own=True, when=inside)
+        send(slot, mine, y_dev, own=True)
+    begin(share_own(mine, c), None)
+
+    for copy in scalar_copies:
+        copy.wait()
     down_copy.wait()
     up_copy.wait()
 
@@ -168,7 +187,6 @@
             copy.start()
         return carry
 
-    lax.fori_loop(1, 16, ship, 0)
     down_in[me] = down_stage[pl.ds(me * per, per)]
     up_in[me] = up_stage[pl.ds(me * per, per)]
     acc[...] = jnp.zeros_like(acc)
@@ -176,25 +194,28 @@
     own_copy.wait()
     tok_copy.wait()
 
+    def ship_all():
+        lax.fori_loop(1, 16, ship, 0)
+
+    def reduce(s, carry):
+        @pl.when(s != me)
+        def _():
+            for copy in adapter_copies(0, me, s):
+                copy.wait_recv()
+
+        cols = pl.ds(pl.multiple_of(s * depth, depth), depth)
+        red[...] += lax.dot_general(
+            tok[:, cols],
+            down_in[s].reshape(per * rank, depth),
+            (((1,), (1,)), ((), ())),
+            preferred_element_type=jnp.float32,
+        )
+        return carry
+
+    def reduces(first, last):
+        return lambda: lax.fori_loop(first, last, reduce, 0)
+
     def adapters():
-        def landed(i, carry):
-            for copy in adapter_copies(i, me, lax.rem(me + 16 - i, 16)):
-                copy.wait_recv()
-            return carry
-
-        lax.fori_loop(1, 16, landed, 0)
-
-        def reduce(s, carry):
-            cols = pl.ds(pl.multiple_of(s * depth, depth), depth)
-            red[...] += lax.dot_general(
-                tok[:, cols],
-                down_in[s].reshape(per * rank, depth),
-                (((1,), (1,)), ((), ())),
-                preferred_element_type=jnp.float32,
-            )
-            return carry
-
-        lax.fori_loop(0, 16, reduce, 0)
         span = rows // per
         row_request = lax.broadcasted_iota(jnp.int32, red.shape, 0) // span
         map_request = lax.broadcasted_iota(jnp.int32, red.shape, 1) // rank
@@ -213,63 +234,97 @@
 
         lax.fori_loop(0, width // 256, tile, 0)
 
-    def from_x(far, k):
-        m = chip(far, k)
-        arrived(2, m, c)
-        send(2, m, sib)
-
-    for k in range(1, 4):
-        near, other = chip(0, k), chip(1, k - 1)
-        for part in (0, 1):
-            arrived(part, near, c)
-            if k == 1:
-                send(part, near, z_in, when=inside)
-            else:
-                send(part, near, z_out, when=inside)
-            send(part, near, y_dev)
-            if part == 0:
-                send(part, near, x_dev, landing=2)
-            send(part, near, sib)
-            arrived(part, other, c)
-            if part == 0:
-                send(part, other, x_dev, landing=2)
-            send(part, other, sib)
-        if k > 1:
-            from_x(0, k - 1)
-            from_x(1, k - 2)
-        if k == 1:
-            sibling_done(mine)
-            multiply(mine)
-        elif k == 2:
-            adapters()
-        else:
-            for far, j in ((0, 1), (1, 0)):
-                sibling_done(chip(far, j))
-                multiply(chip(far, j))
+    def tiles(m, first, last):
+        cols = pl.ds(pl.multiple_of(m * 2 * depth, 2 * depth), 2 * depth)
+
+        def tile(j, carry):
+            at = pl.ds(pl.multiple_of(j * tile_width, tile_width), tile_width)
+            acc[:, at] += jnp.dot(
+                tok[:, cols], wfull[m, :, at], preferred_element_type=jnp.float32
+            )
+            return carry
+
+        lax.fori_loop(first, last, tile, 0)
+
+    crossing = []
+    run = side + mid
+    for k in range(4):
+        for j in range(side):
+            if k < 3:
+                crossing.append((chip(0, k + 1), others[j]))
+            crossing.append((chip(1, k), others[j]))
+
+    def from_x():
+        m, slot = crossing.pop(0)
+        arrived(slot, m, c)
+        send(slot, m, sib)
+
+    def near_strip(k, j):
+        slot, m = (sides + middle)[j], chip(0, k)
+        arrived(slot, m, c)
+        send(slot, m, z_in if k == 1 else z_out, when=inside)
+        send(slot, m, y_dev)
+        if j < side:
+            send(slot, m, x_dev)
+        send(slot, m, sib)
+
+    def far_strip(k, j):
+        slot, m = (sides + middle)[j], chip(1, k)
+        arrived(slot, m, c)
+        if j < side:
+            send(slot, m, x_dev)
+        send(slot, m, sib)
+
+    half = width // tile_width // 2
+    work = {
+        1: lambda: (share_own(mine, 1 - c).wait_recv(), tiles(mine, 0, half)),
+        2: lambda: tiles(mine, half, 2 * half),
+        SHIP: ship_all,
+    }
+    for t, job in REDUCE:
+        work[t] = adapters if job is None else reduces(*job)
+
+    def plan(t, m):
+        work[t] = lambda: (sibling_done(m), tiles(m, 0, half))
+        work[t + 1] = lambda: tiles(m, half, 2 * half)
+
+    for t, far, k in ((8, 0, 1), (10, 1, 0), (13, 0, 2), (15, 1, 1), (19, 0, 3)):
+        plan(t, chip(far, k))
+
+    for t in range(4 * run):
+        if t < 3 * run:
+            near_strip(t // run + 1, t % run)
+        far_strip(t // run, t % run)
+        if t >= 1:
+            from_x()
+        if t + 1 in work:
+            work[t + 1]()
+    while len(crossing) > side:
+        from_x()
+    m = chip(1, 2)
+    sibling_done(m)
+    tiles(m, 0, 2 * half)
+    while crossing:
+        from_x()
     last = chip(1, 3)
-    arrived(0, last, c)
-    send(0, last, x_dev, landing=2)
-    send(0, last, sib)
-    arrived(1, last, c)
-    send(1, last, sib)
-    for far, j in ((0, 3), (1, 2)):
-        from_x(far, j)
-    for far, j in ((0, 2), (1, 1), (0, 3), (1, 2)):
-        sibling_done(chip(far, j))
-        multiply(chip(far, j))
-    from_x(1, 3)
     sibling_done(last)
     cols = pl.ds(pl.multiple_of(last * 2 * depth, 2 * depth), 2 * depth)
+    rows_at = lax.broadcasted_iota(jnp.int32, (rows, 1), 0)
+    bound = jnp.full((rows, 1), len_ref[0], jnp.int32)
+    span = rows // len_count
+    for r in range(1, len_count):
+        bound = jnp.where(rows_at < r * span, bound, len_ref[r] + r * span)
+    live = rows_at < bound
 
     def finish(j, carry):
-        at = pl.ds(pl.multiple_of(j * 256, 256), 256)
+        at = pl.ds(pl.multiple_of(j * tile_width, tile_width), tile_width)
         total = acc[:, at] + jnp.dot(
             tok[:, cols], wfull[last, :, at], preferred_element_type=jnp.float32
         )
-        out_ref[:, at] = total.astype(out_ref.dtype)
-        return carry
-
-    lax.fori_loop(0, width // 256, finish, 0)
+        out_ref[:, at] = jnp.where(live, total, 0.0).astype(out_ref.dtype)
+        return carry
+
+    lax.fori_loop(0, 2 * half, finish, 0)
 
     for copy, when in pending:
         if when is None:
@@ -295,13 +350,15 @@
     part = up.shape[1]
     bf16 = jnp.bfloat16
     any_space = pl.BlockSpec(memory_space=pl.ANY)
-    scalars = pl.BlockSpec(memory_space=pltpu.SMEM)
-    out = pl.pallas_call(
+    return pl.pallas_call(
         gather_kernel,
         out_shape=jax.ShapeDtypeStruct((rows, width), bf16),
-        in_specs=[scalars, scalars] + [any_space] * 4,
+        in_specs=[any_space] * 7,
         out_specs=pl.BlockSpec(memory_space=pltpu.VMEM),
         scratch_shapes=[
+            pltpu.SMEM(request_adapter.shape, jnp.int32),
+            pltpu.SMEM(adapter_table_row.shape, jnp.int32),
+            pltpu.SMEM(lengths.shape, jnp.int32),
             pltpu.VMEM((8, 2 * depth, width), bf16),
             pltpu.VMEM((rows, model), bf16),
             pltpu.VMEM((rows, width), jnp.float32),
@@ -313,14 +370,14 @@
             pltpu.VMEM((16, per, rank, part), bf16),
             pltpu.VMEM((per * rank, width), bf16),
             pltpu.VMEM((rows, per * rank), jnp.float32),
-            pltpu.SemaphoreType.DMA((4,)),
-            pltpu.SemaphoreType.DMA((3, 8, 2)),
-            pltpu.SemaphoreType.DMA((72,)),
+            pltpu.SemaphoreType.DMA((7,)),
+            pltpu.SemaphoreType.DMA((SLOTS, 8, 2)),
+            pltpu.SemaphoreType.DMA((SENDS,)),
             pltpu.SemaphoreType.DMA((2, 16)),
             pltpu.SemaphoreType.DMA((2, 16)),
         ],
         compiler_params=pltpu.CompilerParams(
-            collective_id=0, has_side_effects=True, vmem_limit_bytes=52 * 2**20
+            collective_id=0, has_side_effects=True, vmem_limit_bytes=VM * 2**20
         ),
         cost_estimate=pl.CostEstimate(
             flops=2 * rows * model * width, bytes_accessed=2 * rows * model, transcendentals=0
@@ -328,15 +385,12 @@
     )(
         request_adapter,
         adapter_table_row,
+        lengths,
         tokens,
         weight,
         jnp.swapaxes(down, 1, 2),
         jnp.swapaxes(up, 1, 2),
     )
-    span = rows // per
-    place = jnp.arange(span, dtype=jnp.int32)
-    live = (place[None, :] < lengths[:, None]).reshape(rows, 1)
-    return jnp.where(live, out, jnp.zeros_like(out))
 
 
 def plain_body(

time: 96.6 us -> 87.1 us (0.902)
  Pallas kernels: 92.3 us -> 84.6 us
  other arithmetic: 1.84 us -> 0 us
    pallas_call x1, Pallas kernels: 92.3 us -> 84.6 us  [fused_body(): pl.pallas_call(gather_kernel, out_shape=jax.ShapeDtypeStruct((rows, width...]
    select_n x1 -> x0, other arithmetic: 1.12 us -> none  [fused_body(): return jnp.where(live, out, jnp.zeros_like(out))]
    unnamed x6 -> x1, local copies, waits for them, and re-layouts: 2.26 us -> 2.26 us
where the time goes in v2:
time: 87.1 us; the launch traced here: 86.9 us
  Pallas kernels  84.6 us (97%)
  local copies, waits for them, and re-layouts  2.26 us (3%)
    pallas_call x1, Pallas kernels, fused_body(): pl.pallas_call(gather_kernel, out_shape=jax.ShapeDtypeStruct((rows, width...  84.6 us
    unnamed x1, local copies, waits for them, and re-layouts  2.26 us

profile of v2, /device:TPU:1, one launch (start us, length us, event | category | flops | bytes accessed | tf_op | source)
XLA Modules:
  0.0 86.9 jit_solution(3610602491474594406)
XLA Ops:
  0.0 84.6 %shard_map.73 = bf16[512,1024]{1,0:T(8,128)(2,1)} custom-call(s32[32]{0:T(128)} %req_hbm.1, s32[64]{0:T(128)} %table_hbm.1, s32[2]{0:T(128)} %len_hbm.1, bf16[512,8192]{1,0:T(8,128)(2,1)} %tok_hbm.1, bf16[512,1024]{1,0:T(8,128)(2,1)} %w_hbm.1, bf16[64,16,512]{2,1,0:T(8,128)(2,1)} %bitcast.2, bf16[64,16,64]{2,1,0:T(8,128)(2,1)} %bitcast.3), custom_call_target="tpu_custom_call" | custom-call | flops 8589934592 | bytes 8388608 | tf_op jit(solution)/shard_map/pallas_call | solution.py:353
  84.6 2.3 %copy.9 = bf16[512,1024]{1,0:T(8,128)(2,1)} copy(bf16[512,1024]{1,0:T(8,128)(2,1)} %shard_map.73) | data formatting | bytes 2097152
